TPU v7x, 32 devices: a whole 2x2x4 slice. The times are simulated.
32 devices in a mesh: rows: 8 (over z, y), feat: 4 (over x, core).
Axes of the slice: x: 2, y: 2, z: 4, core: 2. Of those that a mesh axis runs over, the one named last changes fastest.
Arguments:
- bin_codes: int32 [32768, 2048], P('rows', 'feat'), may hold values from 0 to 255
- gradient: bfloat16 [32768], P('rows'), may hold values from -6 to 6
- hessian: bfloat16 [32768], P('rows'), may hold values from 0.049804688 to 1
- leaf_of_block: int32 [256], P('rows'), may hold values from 0 to 1
- block_rows: int32 [256], P('rows'), may hold values from 32 to 128, as said below
Outputs:
- split_gain: float32 [2, 2048, 256], P(None, ('feat', 'rows'))
- best_gain: float32 [2], replicated
Inputs may be any that keep to these rules, and one draw needn't show every extreme that they name: `block_rows`: the live rows are the first ones of their block; some block is full in every draw.
All inputs are finite; a program needn't handle non-finite values.
Results may differ from a plain program's by a relative error of at most 0.0003.
Values sent between devices are 32-bit elements; how exact they have to be, the bound alone decides.
No kernel may reach another device: no remote copies, remote signals or barrier semaphores. Data moves between devices by JAX's collectives and lax.ppermute only.
A program may use at most 64 MiB of HBM per device.

v0:
```python
import math

import jax
import jax.numpy as jnp
from jax import lax
from jax.sharding import PartitionSpec as P

BINS = 256
LEAVES = 2
BLOCK = 128
MIN_CHILD = 20


ridge_term = 1.0


def local(bin_codes, gradient, hessian, leaf_of_block, block_rows):
    row_total, feat_local = bin_codes.shape
    offsets = jnp.arange(row_total, dtype=jnp.int32) % BLOCK
    live_rows = (offsets < jnp.repeat(block_rows, BLOCK)).astype(jnp.float32)
    leaf_ids = jnp.repeat(leaf_of_block, BLOCK)
    leaf_hot = (leaf_ids[:, None] == jnp.arange(LEAVES, dtype=jnp.int32)[None, :]).astype(
        jnp.float32
    ) * live_rows[:, None]
    weights = jnp.concatenate(
        [
            gradient.astype(jnp.float32)[:, None] * leaf_hot,
            hessian.astype(jnp.float32)[:, None] * leaf_hot,
            leaf_hot,
        ],
        1,
    ).astype(jnp.bfloat16)
    bin_values = jnp.arange(BINS, dtype=jnp.int32)
    sub_width = math.gcd(feat_local, 16)

    def sub_block(block_index):
        code_slice = lax.dynamic_slice_in_dim(bin_codes, 0 + block_index * sub_width, sub_width, 1)
        onehot = (code_slice[:, :, None] == bin_values).astype(jnp.bfloat16)
        block_sums = jnp.einsum("rs,rwb->wsb", weights, onehot, preferred_element_type=jnp.float32)
        return block_sums.reshape(sub_width, 3, LEAVES, BINS)

    stacked = lax.map(sub_block, jnp.arange(feat_local // sub_width, dtype=jnp.int32))
    local_sums = stacked.reshape(feat_local, 3, LEAVES, BINS)
    received = lax.all_to_all(local_sums[None], "rows", split_axis=1, concat_axis=0, tiled=True)
    histogram = jnp.sum(received, axis=0)
    running = jnp.cumsum(histogram, axis=3)
    totals = running[..., -1:]
    left_grad, left_hess, left_count = (running[:, 0], running[:, 1], running[:, 2])
    total_grad, total_hess, total_count = (totals[:, 0], totals[:, 1], totals[:, 2])
    right_grad = total_grad - left_grad
    right_hess = total_hess - left_hess
    right_count = total_count - left_count
    raw_gain = 0.5 * (
        left_grad**2 / (left_hess + ridge_term)
        + right_grad**2 / (right_hess + ridge_term)
        - total_grad**2 / (total_hess + ridge_term)
    )
    allowed = (left_count >= MIN_CHILD) & (right_count >= MIN_CHILD)
    split_gain = jnp.transpose(jnp.where(allowed, raw_gain, 0.0), (1, 0, 2))
    best_local = jnp.max(split_gain, axis=(1, 2))
    best_gain = lax.pmax(best_local, ("rows", "feat"))
    return (split_gain, best_gain)


def solution(mesh):
    return jax.shard_map(
        local,
        mesh=mesh,
        in_specs=(P("rows", "feat"), P("rows"), P("rows"), P("rows"), P("rows")),
        out_specs=(P(None, ("feat", "rows"), None), P()),
        check_vma=False,
    )
```

profile of v0, /device:TPU:0, one launch (start us, length us, event | category | flops | bytes accessed | tf_op | source)
XLA Modules:
  0.0 625.0 jit_solution(1631617304164540931)
XLA Ops:
  3.5 8.9 %copy.30 = s32[4096,512]{0,1:T(8,128)} copy(s32[4096,512]{1,0:T(8,128)} %param.7) | data formatting | bytes 16777216
  12.6 486.1 %while.11 = (s32[]{:T(128)}, f32[32,16,3,2,256]{4,1,0,3,2:T(8,128)S(1)}, s32[32]{0:T(128)S(1)}, s32[4096,512]{0,1:T(8,128)}, bf16[4096,6]{0,1:T(8,128)(2,1)S(1)}...) while((s32[]{:T(128)}, f32[32,16,3,2,256]{4,1,0,3,2:T(8,128)S(1)}, s32[32]{0:T(128)S(1)}, ...), condition=%wide.region_1.2_spmd.clone, body=%wide.region_0.1_spmd.clone.sunk | while | flops 218103808 | bytes 1327263 | solution.py:42
  13.8 1.0 constant_dynamic-slice_fusion.2
  14.8 12.9 %fusion.18 = f32[16,6,256]{2,1,0:T(8,128)S(1)} fusion(s32[4096,16]{0,1:T(8,128)S(1)} %constant_dynamic-slice_fusion.2, bf16[4096,6]{0,1:T(8,128)(2,1)S(1)} %get-tuple-element.142), kind=kOutput, calls=%fused_computation.4.clone.2 | convolution fusion | flops 218103808 | bytes 409600 | tf_op jit(solution)/shard_map/while/body/eval_jaxpr/rs,rwb->wsb/dot_general | solution.py:39
  29.0 1.0 constant_dynamic-slice_fusion.2
  30.0 12.9 %fusion.18 = f32[16,6,256]{2,1,0:T(8,128)S(1)} fusion(s32[4096,16]{0,1:T(8,128)S(1)} %constant_dynamic-slice_fusion.2, bf16[4096,6]{0,1:T(8,128)(2,1)S(1)} %get-tuple-element.142), kind=kOutput, calls=%fused_computation.4.clone.2 | convolution fusion | flops 218103808 | bytes 409600 | tf_op jit(solution)/shard_map/while/body/eval_jaxpr/rs,rwb->wsb/dot_general | solution.py:39
  44.2 1.0 constant_dynamic-slice_fusion.2
  45.2 12.9 %fusion.18 = f32[16,6,256]{2,1,0:T(8,128)S(1)} fusion(s32[4096,16]{0,1:T(8,128)S(1)} %constant_dynamic-slice_fusion.2, bf16[4096,6]{0,1:T(8,128)(2,1)S(1)} %get-tuple-element.142), kind=kOutput, calls=%fused_computation.4.clone.2 | convolution fusion | flops 218103808 | bytes 409600 | tf_op jit(solution)/shard_map/while/body/eval_jaxpr/rs,rwb->wsb/dot_general | solution.py:39
  59.4 1.0 constant_dynamic-slice_fusion.2
  60.4 12.9 %fusion.18 = f32[16,6,256]{2,1,0:T(8,128)S(1)} fusion(s32[4096,16]{0,1:T(8,128)S(1)} %constant_dynamic-slice_fusion.2, bf16[4096,6]{0,1:T(8,128)(2,1)S(1)} %get-tuple-element.142), kind=kOutput, calls=%fused_computation.4.clone.2 | convolution fusion | flops 218103808 | bytes 409600 | tf_op jit(solution)/shard_map/while/body/eval_jaxpr/rs,rwb->wsb/dot_general | solution.py:39
  74.6 1.0 constant_dynamic-slice_fusion.2
  75.6 12.9 %fusion.18 = f32[16,6,256]{2,1,0:T(8,128)S(1)} fusion(s32[4096,16]{0,1:T(8,128)S(1)} %constant_dynamic-slice_fusion.2, bf16[4096,6]{0,1:T(8,128)(2,1)S(1)} %get-tuple-element.142), kind=kOutput, calls=%fused_computation.4.clone.2 | convolution fusion | flops 218103808 | bytes 409600 | tf_op jit(solution)/shard_map/while/body/eval_jaxpr/rs,rwb->wsb/dot_general | solution.py:39
  89.8 1.0 constant_dynamic-slice_fusion.2
  90.8 12.9 %fusion.18 = f32[16,6,256]{2,1,0:T(8,128)S(1)} fusion(s32[4096,16]{0,1:T(8,128)S(1)} %constant_dynamic-slice_fusion.2, bf16[4096,6]{0,1:T(8,128)(2,1)S(1)} %get-tuple-element.142), kind=kOutput, calls=%fused_computation.4.clone.2 | convolution fusion | flops 218103808 | bytes 409600 | tf_op jit(solution)/shard_map/while/body/eval_jaxpr/rs,rwb->wsb/dot_general | solution.py:39
  105.0 1.0 constant_dynamic-slice_fusion.2
  105.9 12.9 %fusion.18 = f32[16,6,256]{2,1,0:T(8,128)S(1)} fusion(s32[4096,16]{0,1:T(8,128)S(1)} %constant_dynamic-slice_fusion.2, bf16[4096,6]{0,1:T(8,128)(2,1)S(1)} %get-tuple-element.142), kind=kOutput, calls=%fused_computation.4.clone.2 | convolution fusion | flops 218103808 | bytes 409600 | tf_op jit(solution)/shard_map/while/body/eval_jaxpr/rs,rwb->wsb/dot_general | solution.py:39
  120.2 1.0 constant_dynamic-slice_fusion.2
  121.1 12.9 %fusion.18 = f32[16,6,256]{2,1,0:T(8,128)S(1)} fusion(s32[4096,16]{0,1:T(8,128)S(1)} %constant_dynamic-slice_fusion.2, bf16[4096,6]{0,1:T(8,128)(2,1)S(1)} %get-tuple-element.142), kind=kOutput, calls=%fused_computation.4.clone.2 | convolution fusion | flops 218103808 | bytes 409600 | tf_op jit(solution)/shard_map/while/body/eval_jaxpr/rs,rwb->wsb/dot_general | solution.py:39
  135.4 1.0 constant_dynamic-slice_fusion.2
  136.3 12.9 %fusion.18 = f32[16,6,256]{2,1,0:T(8,128)S(1)} fusion(s32[4096,16]{0,1:T(8,128)S(1)} %constant_dynamic-slice_fusion.2, bf16[4096,6]{0,1:T(8,128)(2,1)S(1)} %get-tuple-element.142), kind=kOutput, calls=%fused_computation.4.clone.2 | convolution fusion | flops 218103808 | bytes 409600 | tf_op jit(solution)/shard_map/while/body/eval_jaxpr/rs,rwb->wsb/dot_general | solution.py:39
  150.5 1.0 constant_dynamic-slice_fusion.2
  151.5 12.9 %fusion.18 = f32[16,6,256]{2,1,0:T(8,128)S(1)} fusion(s32[4096,16]{0,1:T(8,128)S(1)} %constant_dynamic-slice_fusion.2, bf16[4096,6]{0,1:T(8,128)(2,1)S(1)} %get-tuple-element.142), kind=kOutput, calls=%fused_computation.4.clone.2 | convolution fusion | flops 218103808 | bytes 409600 | tf_op jit(solution)/shard_map/while/body/eval_jaxpr/rs,rwb->wsb/dot_general | solution.py:39
  165.7 1.0 constant_dynamic-slice_fusion.2
  166.7 12.9 %fusion.18 = f32[16,6,256]{2,1,0:T(8,128)S(1)} fusion(s32[4096,16]{0,1:T(8,128)S(1)} %constant_dynamic-slice_fusion.2, bf16[4096,6]{0,1:T(8,128)(2,1)S(1)} %get-tuple-element.142), kind=kOutput, calls=%fused_computation.4.clone.2 | convolution fusion | flops 218103808 | bytes 409600 | tf_op jit(solution)/shard_map/while/body/eval_jaxpr/rs,rwb->wsb/dot_general | solution.py:39
  180.9 1.0 constant_dynamic-slice_fusion.2
  181.9 12.9 %fusion.18 = f32[16,6,256]{2,1,0:T(8,128)S(1)} fusion(s32[4096,16]{0,1:T(8,128)S(1)} %constant_dynamic-slice_fusion.2, bf16[4096,6]{0,1:T(8,128)(2,1)S(1)} %get-tuple-element.142), kind=kOutput, calls=%fused_computation.4.clone.2 | convolution fusion | flops 218103808 | bytes 409600 | tf_op jit(solution)/shard_map/while/body/eval_jaxpr/rs,rwb->wsb/dot_general | solution.py:39
  196.1 1.0 constant_dynamic-slice_fusion.2
  197.1 12.9 %fusion.18 = f32[16,6,256]{2,1,0:T(8,128)S(1)} fusion(s32[4096,16]{0,1:T(8,128)S(1)} %constant_dynamic-slice_fusion.2, bf16[4096,6]{0,1:T(8,128)(2,1)S(1)} %get-tuple-element.142), kind=kOutput, calls=%fused_computation.4.clone.2 | convolution fusion | flops 218103808 | bytes 409600 | tf_op jit(solution)/shard_map/while/body/eval_jaxpr/rs,rwb->wsb/dot_general | solution.py:39
  211.3 1.0 constant_dynamic-slice_fusion.2
  212.3 12.9 %fusion.18 = f32[16,6,256]{2,1,0:T(8,128)S(1)} fusion(s32[4096,16]{0,1:T(8,128)S(1)} %constant_dynamic-slice_fusion.2, bf16[4096,6]{0,1:T(8,128)(2,1)S(1)} %get-tuple-element.142), kind=kOutput, calls=%fused_computation.4.clone.2 | convolution fusion | flops 218103808 | bytes 409600 | tf_op jit(solution)/shard_map/while/body/eval_jaxpr/rs,rwb->wsb/dot_general | solution.py:39
  226.5 1.0 constant_dynamic-slice_fusion.2
  227.5 12.9 %fusion.18 = f32[16,6,256]{2,1,0:T(8,128)S(1)} fusion(s32[4096,16]{0,1:T(8,128)S(1)} %constant_dynamic-slice_fusion.2, bf16[4096,6]{0,1:T(8,128)(2,1)S(1)} %get-tuple-element.142), kind=kOutput, calls=%fused_computation.4.clone.2 | convolution fusion | flops 218103808 | bytes 409600 | tf_op jit(solution)/shard_map/while/body/eval_jaxpr/rs,rwb->wsb/dot_general | solution.py:39
  241.7 1.0 constant_dynamic-slice_fusion.2
  242.7 12.9 %fusion.18 = f32[16,6,256]{2,1,0:T(8,128)S(1)} fusion(s32[4096,16]{0,1:T(8,128)S(1)} %constant_dynamic-slice_fusion.2, bf16[4096,6]{0,1:T(8,128)(2,1)S(1)} %get-tuple-element.142), kind=kOutput, calls=%fused_computation.4.clone.2 | convolution fusion | flops 218103808 | bytes 409600 | tf_op jit(solution)/shard_map/while/body/eval_jaxpr/rs,rwb->wsb/dot_general | solution.py:39
  256.9 1.0 constant_dynamic-slice_fusion.2
  257.8 12.9 %fusion.18 = f32[16,6,256]{2,1,0:T(8,128)S(1)} fusion(s32[4096,16]{0,1:T(8,128)S(1)} %constant_dynamic-slice_fusion.2, bf16[4096,6]{0,1:T(8,128)(2,1)S(1)} %get-tuple-element.142), kind=kOutput, calls=%fused_computation.4.clone.2 | convolution fusion | flops 218103808 | bytes 409600 | tf_op jit(solution)/shard_map/while/body/eval_jaxpr/rs,rwb->wsb/dot_general | solution.py:39
  272.1 1.0 constant_dynamic-slice_fusion.2
  273.0 12.9 %fusion.18 = f32[16,6,256]{2,1,0:T(8,128)S(1)} fusion(s32[4096,16]{0,1:T(8,128)S(1)} %constant_dynamic-slice_fusion.2, bf16[4096,6]{0,1:T(8,128)(2,1)S(1)} %get-tuple-element.142), kind=kOutput, calls=%fused_computation.4.clone.2 | convolution fusion | flops 218103808 | bytes 409600 | tf_op jit(solution)/shard_map/while/body/eval_jaxpr/rs,rwb->wsb/dot_general | solution.py:39
  287.3 1.0 constant_dynamic-slice_fusion.2
  288.2 12.9 %fusion.18 = f32[16,6,256]{2,1,0:T(8,128)S(1)} fusion(s32[4096,16]{0,1:T(8,128)S(1)} %constant_dynamic-slice_fusion.2, bf16[4096,6]{0,1:T(8,128)(2,1)S(1)} %get-tuple-element.142), kind=kOutput, calls=%fused_computation.4.clone.2 | convolution fusion | flops 218103808 | bytes 409600 | tf_op jit(solution)/shard_map/while/body/eval_jaxpr/rs,rwb->wsb/dot_general | solution.py:39
  302.4 1.0 constant_dynamic-slice_fusion.2
  303.4 12.9 %fusion.18 = f32[16,6,256]{2,1,0:T(8,128)S(1)} fusion(s32[4096,16]{0,1:T(8,128)S(1)} %constant_dynamic-slice_fusion.2, bf16[4096,6]{0,1:T(8,128)(2,1)S(1)} %get-tuple-element.142), kind=kOutput, calls=%fused_computation.4.clone.2 | convolution fusion | flops 218103808 | bytes 409600 | tf_op jit(solution)/shard_map/while/body/eval_jaxpr/rs,rwb->wsb/dot_general | solution.py:39
  317.6 1.0 constant_dynamic-slice_fusion.2
  318.6 12.9 %fusion.18 = f32[16,6,256]{2,1,0:T(8,128)S(1)} fusion(s32[4096,16]{0,1:T(8,128)S(1)} %constant_dynamic-slice_fusion.2, bf16[4096,6]{0,1:T(8,128)(2,1)S(1)} %get-tuple-element.142), kind=kOutput, calls=%fused_computation.4.clone.2 | convolution fusion | flops 218103808 | bytes 409600 | tf_op jit(solution)/shard_map/while/body/eval_jaxpr/rs,rwb->wsb/dot_general | solution.py:39
  332.8 1.0 constant_dynamic-slice_fusion.2
  333.8 12.9 %fusion.18 = f32[16,6,256]{2,1,0:T(8,128)S(1)} fusion(s32[4096,16]{0,1:T(8,128)S(1)} %constant_dynamic-slice_fusion.2, bf16[4096,6]{0,1:T(8,128)(2,1)S(1)} %get-tuple-element.142), kind=kOutput, calls=%fused_computation.4.clone.2 | convolution fusion | flops 218103808 | bytes 409600 | tf_op jit(solution)/shard_map/while/body/eval_jaxpr/rs,rwb->wsb/dot_general | solution.py:39
  348.0 1.0 constant_dynamic-slice_fusion.2
  349.0 12.9 %fusion.18 = f32[16,6,256]{2,1,0:T(8,128)S(1)} fusion(s32[4096,16]{0,1:T(8,128)S(1)} %constant_dynamic-slice_fusion.2, bf16[4096,6]{0,1:T(8,128)(2,1)S(1)} %get-tuple-element.142), kind=kOutput, calls=%fused_computation.4.clone.2 | convolution fusion | flops 218103808 | bytes 409600 | tf_op jit(solution)/shard_map/while/body/eval_jaxpr/rs,rwb->wsb/dot_general | solution.py:39
  363.2 1.0 constant_dynamic-slice_fusion.2
  364.2 12.9 %fusion.18 = f32[16,6,256]{2,1,0:T(8,128)S(1)} fusion(s32[4096,16]{0,1:T(8,128)S(1)} %constant_dynamic-slice_fusion.2, bf16[4096,6]{0,1:T(8,128)(2,1)S(1)} %get-tuple-element.142), kind=kOutput, calls=%fused_computation.4.clone.2 | convolution fusion | flops 218103808 | bytes 409600 | tf_op jit(solution)/shard_map/while/body/eval_jaxpr/rs,rwb->wsb/dot_general | solution.py:39
  378.4 1.0 constant_dynamic-slice_fusion.2
  379.4 12.9 %fusion.18 = f32[16,6,256]{2,1,0:T(8,128)S(1)} fusion(s32[4096,16]{0,1:T(8,128)S(1)} %constant_dynamic-slice_fusion.2, bf16[4096,6]{0,1:T(8,128)(2,1)S(1)} %get-tuple-element.142), kind=kOutput, calls=%fused_computation.4.clone.2 | convolution fusion | flops 218103808 | bytes 409600 | tf_op jit(solution)/shard_map/while/body/eval_jaxpr/rs,rwb->wsb/dot_general | solution.py:39
  394.6 12.9 %fusion.18 = f32[16,6,256]{2,1,0:T(8,128)S(1)} fusion(s32[4096,16]{0,1:T(8,128)S(1)} %constant_dynamic-slice_fusion.2, bf16[4096,6]{0,1:T(8,128)(2,1)S(1)} %get-tuple-element.142), kind=kOutput, calls=%fused_computation.4.clone.2 | convolution fusion | flops 218103808 | bytes 409600 | tf_op jit(solution)/shard_map/while/body/eval_jaxpr/rs,rwb->wsb/dot_general | solution.py:39
  409.7 12.9 %fusion.18 = f32[16,6,256]{2,1,0:T(8,128)S(1)} fusion(s32[4096,16]{0,1:T(8,128)S(1)} %constant_dynamic-slice_fusion.2, bf16[4096,6]{0,1:T(8,128)(2,1)S(1)} %get-tuple-element.142), kind=kOutput, calls=%fused_computation.4.clone.2 | convolution fusion | flops 218103808 | bytes 409600 | tf_op jit(solution)/shard_map/while/body/eval_jaxpr/rs,rwb->wsb/dot_general | solution.py:39
  424.9 12.9 %fusion.18 = f32[16,6,256]{2,1,0:T(8,128)S(1)} fusion(s32[4096,16]{0,1:T(8,128)S(1)} %constant_dynamic-slice_fusion.2, bf16[4096,6]{0,1:T(8,128)(2,1)S(1)} %get-tuple-element.142), kind=kOutput, calls=%fused_computation.4.clone.2 | convolution fusion | flops 218103808 | bytes 409600 | tf_op jit(solution)/shard_map/while/body/eval_jaxpr/rs,rwb->wsb/dot_general | solution.py:39
  440.1 12.9 %fusion.18 = f32[16,6,256]{2,1,0:T(8,128)S(1)} fusion(s32[4096,16]{0,1:T(8,128)S(1)} %constant_dynamic-slice_fusion.2, bf16[4096,6]{0,1:T(8,128)(2,1)S(1)} %get-tuple-element.142), kind=kOutput, calls=%fused_computation.4.clone.2 | convolution fusion | flops 218103808 | bytes 409600 | tf_op jit(solution)/shard_map/while/body/eval_jaxpr/rs,rwb->wsb/dot_general | solution.py:39
  455.3 12.9 %fusion.18 = f32[16,6,256]{2,1,0:T(8,128)S(1)} fusion(s32[4096,16]{0,1:T(8,128)S(1)} %constant_dynamic-slice_fusion.2, bf16[4096,6]{0,1:T(8,128)(2,1)S(1)} %get-tuple-element.142), kind=kOutput, calls=%fused_computation.4.clone.2 | convolution fusion | flops 218103808 | bytes 409600 | tf_op jit(solution)/shard_map/while/body/eval_jaxpr/rs,rwb->wsb/dot_general | solution.py:39
  470.5 12.9 %fusion.18 = f32[16,6,256]{2,1,0:T(8,128)S(1)} fusion(s32[4096,16]{0,1:T(8,128)S(1)} %constant_dynamic-slice_fusion.2, bf16[4096,6]{0,1:T(8,128)(2,1)S(1)} %get-tuple-element.142), kind=kOutput, calls=%fused_computation.4.clone.2 | convolution fusion | flops 218103808 | bytes 409600 | tf_op jit(solution)/shard_map/while/body/eval_jaxpr/rs,rwb->wsb/dot_general | solution.py:39
  485.7 12.9 %fusion.18 = f32[16,6,256]{2,1,0:T(8,128)S(1)} fusion(s32[4096,16]{0,1:T(8,128)S(1)} %constant_dynamic-slice_fusion.2, bf16[4096,6]{0,1:T(8,128)(2,1)S(1)} %get-tuple-element.142), kind=kOutput, calls=%fused_computation.4.clone.2 | convolution fusion | flops 218103808 | bytes 409600 | tf_op jit(solution)/shard_map/while/body/eval_jaxpr/rs,rwb->wsb/dot_general | solution.py:39
  498.7 2.4 copy.32
  501.1 77.8 %all_to_all.12 = f32[1,512,3,2,256]{4,3,2,0,1:T(2,128)S(1)} all-to-all(f32[1,512,3,2,256]{4,3,2,0,1:T(2,128)S(1)} %copy.32), channel_id=1, replica_groups=mesh['rows'=8,'feat'=4] {'rows'}, dimensions={1} | all-to-all | bytes 6291456 | tf_op jit(solution)/shard_map/all_to_all | solution.py:44
  578.9 1.7 reduce_sum.9
  581.1 3.6 reduce-window.6
  586.3 38.8 %pmax.7 = f32[2]{0:T(128)} all-reduce(f32[2]{0:T(128)S(1)} %get-tuple-element.85), channel_id=1, replica_groups=mesh['rows'=8,'feat'=4] {'rows','feat'}, use_global_device_ids=true, to_apply=%region_6.7 | all-reduce | flops 2 | bytes 16 | tf_op jit(solution)/shard_map/pmax | solution.py:61
  (125 shorter events, 32.4 us)
Async XLA Ops:
  0.6 0.7 copy-start
where the time goes:
time: 627 us; the launch traced here: 625 us
  matrix products  412 us (66%)
  blocking collectives  117 us (19%)
  local copies, waits for them, and re-layouts  64.8 us (10%)
  loops' own time  22.1 us (4%)
  other arithmetic  8.53 us (1%)
    dot_general x32, matrix products, sub_block(): jnp.einsum('rs,rwb->wsb', weights, onehot, preferred_element_type=jnp.flo...  412 us
    all_to_all x1, blocking collectives, local(): lax.all_to_all(local_sums[None], 'rows', split_axis=1, concat_axis=0, til...  77.8 us
    pmax x1, blocking collectives, local(): best_gain = lax.pmax(best_local, ('rows', 'feat'))  38.8 us
    dynamic_slice x32, local copies, waits for them, and re-layouts, sub_block(): lax.dynamic_slice_in_dim(bin_codes, 0 + block_index * sub_width, sub_widt...  31.1 us
    another operation x1, loops' own time, local(): lax.map(sub_block, jnp.arange(feat_local // sub_width, dtype=jnp.int32))  22.1 us
    dynamic_slice x32, local copies, waits for them, and re-layouts, local(): lax.map(sub_block, jnp.arange(feat_local // sub_width, dtype=jnp.int32))  18.8 us

commit v1 on v0

v1 whole, which is shorter than its diff:
```python
import functools

import jax
import jax.numpy as jnp
from jax import lax
from jax.experimental import pallas as pl
from jax.experimental.pallas import tpu as pltpu
from jax.sharding import PartitionSpec as P

BINS = 256
LEAVES = 2
BLOCK = 128
MIN_CHILD = 20
RIDGE = 1.0

STATS = 3
HIGH = 8
LOW = 32
FOLD = 8
PAIR = 2 * FOLD
WIDTH = LOW * FOLD
DEPTH = STATS * HIGH * FOLD
BIG = 1024
SMALL = 256
SPAN = 512
WAYS = 4

BF = jnp.bfloat16
F32 = jnp.float32
VMEM_BYTES = 56 << 20


def nt(a, b):
    return lax.dot_general(a, b, (((1,), (1,)), ((), ())), preferred_element_type=F32)


def exact(a, b):
    return lax.dot_general(
        a, b, (((1,), (0,)), ((), ())), precision=lax.Precision.HIGHEST, preferred_element_type=F32
    )


def live_up(count):
    return (count + 15) // 16 * 16


def pack_kernel(
    steps, blocks, pos_ref, leaf_ref, rows_ref, codes_ref, stats_ref, table_ref, weight_ref, info_ref, held, rows_held, offset
):
    step = pl.program_id(0)
    per_step = SPAN // BLOCK

    @pl.when(step == 0)
    def _():
        def count(k, ends):
            room = live_up(rows_ref[k])
            second = leaf_ref[k]
            return ends[0] + room * (1 - second), ends[1] + room * second

        first, second = lax.fori_loop(0, blocks, count, (0, 0))
        start = (first + SMALL - 1) // SMALL * SMALL + BLOCK

        def place(k, ends):
            room = live_up(rows_ref[k])
            leaf = leaf_ref[k]
            offset[k] = jnp.where(leaf == 0, ends[0], ends[1])
            return ends[0] + room * (1 - leaf), ends[1] + room * leaf

        lax.fori_loop(0, blocks, place, (0, start))
        for leaf, total in ((0, first), (1, second)):
            tiles = (total + SMALL - 1) // SMALL
            info_ref[2 * leaf] = tiles // (BIG // SMALL)
            info_ref[2 * leaf + 1] = tiles % (BIG // SMALL)
        info_ref[4] = start
        info_ref[5] = pos_ref[0]
        info_ref[6] = start + (second + SMALL - 1) // SMALL * SMALL
        info_ref[7] = 0
        rows_held[...] = jnp.zeros_like(rows_held)

    @pl.when(step < steps)
    def _():
        lane = lax.broadcasted_iota(jnp.int32, (8, BLOCK), 1)
        row = lax.broadcasted_iota(jnp.int32, (8, BLOCK), 0)
        for i in range(per_step):
            k = step * per_step + i
            at = pl.multiple_of(offset[k], 16)
            held[pl.ds(at, BLOCK), :] = codes_ref[i * BLOCK : (i + 1) * BLOCK, :].astype(F32).astype(BF)
            grad = jnp.broadcast_to(stats_ref[0, pl.ds(k, 1), :], (8, BLOCK))
            hess = jnp.broadcast_to(stats_ref[1, pl.ds(k, 1), :], (8, BLOCK))
            value = jnp.where(row == 0, grad, jnp.where(row == 1, hess, jnp.where(row == 2, 1.0, 0.0)))
            value = jnp.where(lane < rows_ref[k], value, 0.0)
            shift = lax.rem(at, BLOCK)
            tile = pl.multiple_of(at - shift, BLOCK)
            turned = pltpu.roll(value, shift, 1)
            here = rows_held[:, pl.ds(tile, BLOCK)]
            rows_held[:, pl.ds(tile, BLOCK)] = jnp.where(lane < shift, here, turned)
            rows_held[:, pl.ds(pl.multiple_of(tile + BLOCK, BLOCK), BLOCK)] = jnp.where(lane < shift, turned, 0.0)

    @pl.when(step >= steps)
    def _():
        at = pl.multiple_of((step - steps) * SPAN, SPAN)

        @pl.when(at < info_ref[6])
        def _():
            size = 256
            eye = (
                lax.broadcasted_iota(jnp.int32, (size, size), 0) == lax.broadcasted_iota(jnp.int32, (size, size), 1)
            ).astype(F32).astype(BF)
            for f in range(0, table_ref.shape[0], size):
                table_ref[f : f + size, :] = nt(eye, held[pl.ds(at, SPAN), f : f + size]).astype(BF)
            for s in range(STATS):
                weight_ref[s] = jnp.broadcast_to(rows_held[s : s + 1, pl.ds(at, SPAN)], (16, SPAN)).astype(BF)


def pack(pos, leaf_of_block, block_rows, codes, stats, room):
    row_total, feat_local = codes.shape
    blocks = row_total // BLOCK
    steps = row_total // SPAN
    return pl.pallas_call(
        functools.partial(pack_kernel, steps, blocks),
        grid_spec=pltpu.PrefetchScalarGridSpec(
            num_scalar_prefetch=3,
            grid=(steps + room // SPAN,),
            in_specs=[
                pl.BlockSpec((SPAN, feat_local), lambda i, *_: (jnp.minimum(i, steps - 1), 0)),
                pl.BlockSpec((2, blocks, BLOCK), lambda i, *_: (0, 0, 0)),
            ],
            out_specs=[
                pl.BlockSpec((feat_local, SPAN), lambda i, *_: (0, jnp.maximum(i - steps, 0))),
                pl.BlockSpec((STATS, 16, SPAN), lambda i, *_: (0, 0, jnp.maximum(i - steps, 0))),
                pl.BlockSpec(memory_space=pltpu.SMEM),
            ],
            scratch_shapes=[
                pltpu.VMEM((room, feat_local), BF),
                pltpu.VMEM((8, room), F32),
                pltpu.SMEM((blocks,), jnp.int32),
            ],
        ),
        out_shape=[
            jax.ShapeDtypeStruct((feat_local, room), BF),
            jax.ShapeDtypeStruct((STATS, 16, room), BF),
            jax.ShapeDtypeStruct((8,), jnp.int32),
        ],
        compiler_params=pltpu.CompilerParams(vmem_limit_bytes=VMEM_BYTES),
        cost_estimate=pl.CostEstimate(flops=4 << 30, bytes_accessed=16 << 20, transcendentals=0),
    )(pos, leaf_of_block, block_rows, codes, stats)


def histogram_kernel(add, *refs):
    info_ref = refs[0]
    tables = refs[1 : 1 + WAYS]
    weight_ref = refs[1 + WAYS]
    if add:
        recv_ref = refs[2 + WAYS]
        outs, total = refs[3 + WAYS : 3 + 2 * WAYS], refs[3 + 2 * WAYS]
    else:
        outs, total = refs[2 + WAYS : 3 + WAYS], refs[3 + WAYS]
    folds = 2 * WAYS
    lane = lax.broadcasted_iota(jnp.int32, (FOLD, WIDTH), 1)
    skew = (lax.broadcasted_iota(jnp.int32, (FOLD, WIDTH), 0) - lane) & (FOLD - 1)

    def product(at, size):
        half = (lax.broadcasted_iota(jnp.int32, (16, size), 0) // FOLD).astype(F32).astype(BF)
        one, zero = jnp.ones((16, size), BF), jnp.zeros((16, size), BF)
        weights = [weight_ref[s, :, pl.ds(at, size)] for s in range(STATS)]
        for way in range(WAYS):
            both = tables[way][:, pl.ds(at, size)].astype(F32)
            for i in range(2):
                code = both[i * FOLD : (i + 1) * FOLD]
                high = jnp.floor(code * (1.0 / LOW))
                low = code - high * LOW
                high = jnp.concatenate([high, high], 0).astype(BF) - half
                low = jnp.concatenate([low, low], 0).astype(BF) - half
                picks = jnp.concatenate([jnp.where(low == BF(2 * q), one, zero) for q in range(LOW // 2)], 0)
                masks = [high == BF(2 * q) for q in range(HIGH // 2)]
                terms = jnp.concatenate([jnp.where(m, w, zero) for w in weights for m in masks], 0)
                total[2 * way + i] += nt(terms, picks)

    for leaf in range(LEAVES):
        total[...] = jnp.zeros_like(total)
        start = info_ref[4] if leaf else 0
        big, small = info_ref[2 * leaf], info_ref[2 * leaf + 1]

        @pl.loop(0, big)
        def _(k):
            product(pl.multiple_of(start + k * BIG, BLOCK), BIG)

        @pl.loop(0, small)
        def _(k):
            product(pl.multiple_of(start + big * BIG + k * SMALL, BLOCK), SMALL)

        for way in range(WAYS):
            for i in range(2):
                for s in range(STATS):
                    base = s * HIGH * FOLD
                    value = total[2 * way + i, base : base + FOLD]
                    for h in range(1, HIGH):
                        piece = total[2 * way + i, base + h * FOLD : base + (h + 1) * FOLD]
                        value = jnp.where(skew == h, pltpu.roll(piece, h, 0), value)
                    if add:
                        outs[way][i, leaf, s] = value + recv_ref[way, i, leaf, s]
                    else:
                        outs[0][way, i, leaf, s] = value


def histogram(info, table, weight, owners, chunk, ways, other, recv):
    room = table.shape[1]
    per_owner = table.shape[0] // owners // PAIR
    add = recv is not None

    def at(way):
        def index(i, info):
            pos = info[5]
            owner = ((pos // 2) ^ way) * 2 + ((pos & 1) ^ other)
            return owner * per_owner + chunk, 0

        return index

    block = (2, LEAVES, STATS, FOLD, WIDTH)
    if add:
        out_shape = [jax.ShapeDtypeStruct(block, F32)] * WAYS
        out_specs = [pl.BlockSpec(block, lambda i, info: (0,) * 5)] * WAYS
    else:
        out_shape = [jax.ShapeDtypeStruct((WAYS,) + block, F32)]
        out_specs = [pl.BlockSpec((WAYS,) + block, lambda i, info: (0,) * 6)]
    return pl.pallas_call(
        functools.partial(histogram_kernel, add),
        grid_spec=pltpu.PrefetchScalarGridSpec(
            num_scalar_prefetch=1,
            grid=(1,),
            in_specs=[pl.BlockSpec((PAIR, room), at(way)) for way in ways]
            + [pl.BlockSpec((STATS, 16, room), lambda i, info: (0, 0, 0))]
            + ([pl.BlockSpec((WAYS,) + block, lambda i, info: (0,) * 6)] if add else []),
            out_specs=out_specs,
            scratch_shapes=[pltpu.VMEM((2 * WAYS, DEPTH, WIDTH), F32)],
        ),
        out_shape=out_shape,
        compiler_params=pltpu.CompilerParams(vmem_limit_bytes=VMEM_BYTES),
        cost_estimate=pl.CostEstimate(flops=6 << 30, bytes_accessed=4 << 20, transcendentals=0),
    )(info, *([table] * WAYS), weight, *([recv] if add else []))


def gain_kernel(parts, *refs):
    own = refs[:parts]
    best_ref = refs[parts + 1]
    gain_ref, top_ref = refs[parts + 2], refs[parts + 3]
    lane = lax.broadcasted_iota(jnp.int32, (FOLD, WIDTH), 1)
    row = lax.broadcasted_iota(jnp.int32, (FOLD, WIDTH), 0)
    rows = lax.broadcasted_iota(jnp.int32, (WIDTH, WIDTH), 0)
    cols = lax.broadcasted_iota(jnp.int32, (WIDTH, WIDTH), 1)
    same = (rows % FOLD) == (cols % FOLD)
    upto = (same & (rows // FOLD <= cols // FOLD)).astype(F32)
    same = same.astype(F32)
    order = ((rows % FOLD == cols // LOW) & (rows // FOLD == cols % LOW)).astype(F32)
    pieces = []
    for i in range(2):
        for leaf in range(LEAVES):
            for s in range(STATS):
                x = own[0][i, leaf, s]
                for p in range(1, parts):
                    x = x + own[p][i, leaf, s]
                for bit in (1, 2, 4):
                    x = jnp.where((lane & bit) != 0, pltpu.roll(x, FOLD - bit, 0), x)
                pieces.append(x)
    stacked = jnp.concatenate(pieces, 0)
    inner = exact(stacked, upto)
    whole = exact(stacked, same)
    gains = []
    for i in range(2):
        for leaf in range(LEAVES):
            left, total = [], []
            for s in range(STATS):
                at = ((i * LEAVES + leaf) * STATS + s) * FOLD
                sums = whole[at : at + FOLD]
                run = sums
                for step in (1, 2, 4):
                    run = run + jnp.where(row >= step, pltpu.roll(run, step, 0), 0.0)
                before = jnp.where(row >= 1, pltpu.roll(run, 1, 0), 0.0)
                left.append(inner[at : at + FOLD] + before)
                total.append(jnp.broadcast_to(run[FOLD - 1 : FOLD], (FOLD, WIDTH)))
            right = [t - a for t, a in zip(total, left)]
            raw = 0.5 * (
                left[0] * left[0] / (left[1] + RIDGE)
                + right[0] * right[0] / (right[1] + RIDGE)
                - total[0] * total[0] / (total[1] + RIDGE)
            )
            gains.append(jnp.where((left[2] >= MIN_CHILD) & (right[2] >= MIN_CHILD), raw, 0.0))
    turned = exact(jnp.concatenate(gains, 0), order)
    for i in range(2):
        for leaf in range(LEAVES):
            at = (i * LEAVES + leaf) * FOLD
            z = turned[at : at + FOLD]
            out = jnp.where(((row - lane // LOW) & (FOLD - 1)) == 0, z, 0.0)
            for d in range(1, FOLD):
                part = jnp.where(((row - lane // LOW) & (FOLD - 1)) == d, z, 0.0)
                out = out + pltpu.roll(pltpu.roll(part, FOLD - d, 0), LOW * d, 1)
            gain_ref[leaf, i * FOLD : (i + 1) * FOLD, :] = out
    tops = [
        jnp.max(jnp.maximum(gains[leaf], gains[LEAVES + leaf]), axis=(0, 1), keepdims=True) for leaf in range(LEAVES)
    ]
    at = lax.broadcasted_iota(jnp.int32, top_ref.shape, 1)
    top_ref[...] = jnp.maximum(best_ref[...], jnp.where(at == 0, tops[0], tops[1]))


def gain(parts, chunk, split_gain, best):
    block = (2, LEAVES, STATS, FOLD, WIDTH)
    count = len(parts)
    return pl.pallas_call(
        functools.partial(gain_kernel, count),
        grid=(1,),
        in_specs=[pl.BlockSpec(block, lambda i: (0,) * 5)] * count
        + [pl.BlockSpec(memory_space=pl.ANY), pl.BlockSpec(best.shape, lambda i: (0, 0))],
        out_specs=[
            pl.BlockSpec((LEAVES, PAIR, BINS), lambda i: (0, chunk, 0)),
            pl.BlockSpec(best.shape, lambda i: (0, 0)),
        ],
        out_shape=[
            jax.ShapeDtypeStruct(split_gain.shape, F32),
            jax.ShapeDtypeStruct(best.shape, F32),
        ],
        input_output_aliases={count: 0, count + 1: 1},
        compiler_params=pltpu.CompilerParams(vmem_limit_bytes=VMEM_BYTES),
    )(*parts, split_gain, best)


def local(owners, devices, bin_codes, gradient, hessian, leaf_of_block, block_rows):
    row_total, feat_local = bin_codes.shape
    blocks = row_total // BLOCK
    pos = lax.axis_index("rows").astype(jnp.int32)[None]
    stats = jnp.stack([gradient.reshape(blocks, BLOCK), hessian.reshape(blocks, BLOCK)]).astype(F32)
    room = -(-(row_total + 2 * SMALL + BLOCK) // SPAN) * SPAN
    table, weight, info = pack(pos, leaf_of_block, block_rows, bin_codes, stats, room)
    chunks = feat_local // owners // PAIR
    sides = owners // 2
    swap = [(i, i ^ 1) for i in range(owners)]
    split_gain = jnp.zeros((LEAVES, feat_local // owners, BINS), F32)
    best = jnp.full((devices, 128), -jnp.inf, F32)

    def to_partner(chunk):
        return [
            lax.ppermute(
                histogram(info, table, weight, owners, chunk, range(base, base + WAYS), 1, None)[0], "rows", swap
            )
            for base in range(0, sides, WAYS)
        ]

    received = {0: to_partner(0)}
    for chunk in range(chunks):
        if chunk + 1 < chunks:
            received[chunk + 1] = to_partner(chunk + 1)
        mine = []
        for base in range(0, sides, WAYS):
            mine += histogram(
                info, table, weight, owners, chunk, range(base, base + WAYS), 0, received[chunk][base // WAYS]
            )
        parts = [mine[0]]
        for way in range(1, sides):
            parts.append(lax.ppermute(mine[way], "rows", [(i, i ^ (2 * way)) for i in range(owners)]))
        split_gain, best = gain(parts, chunk, split_gain, best)
    best = lax.all_to_all(best, ("rows", "feat"), 0, 0, tiled=True)
    return split_gain, jnp.max(best, axis=0)[:LEAVES]


def solution(mesh):
    return jax.shard_map(
        functools.partial(local, mesh.shape["rows"], mesh.size),
        mesh=mesh,
        in_specs=(P("rows", "feat"), P("rows"), P("rows"), P("rows"), P("rows")),
        out_specs=(P(None, ("feat", "rows"), None), P()),
        check_vma=False,
    )
```

time: 627 us -> 131 us (0.21)
  matrix products: 412 us -> 0 us
  blocking collectives: 117 us -> 11.5 us
  Pallas kernels: 0 us -> 89.9 us
  local copies, waits for them, and re-layouts: 64.8 us -> 4.59 us
  starting transfers between devices: 0 us -> 22.2 us
  loops' own time: 22.1 us -> 0 us
  other arithmetic: 8.53 us -> 1.89 us
    dot_general x32 -> x0, matrix products: 412 us -> none  [sub_block(): jnp.einsum('rs,rwb->wsb', weights, onehot, preferred_element_type=jnp.flo...]
    pallas_call x0 -> x13, Pallas kernels: none -> 89.9 us  [the longest x8 66.8 us: histogram(): pl.pallas_call(functools.partial(histogram_kernel, add), grid_spec=pltpu....]
    all_to_all x1, blocking collectives: 77.8 us -> 11.5 us  [local(): best = lax.all_to_all(best, ('rows', 'feat'), 0, 0, tiled=True)]
    dynamic_slice x64 -> x0, local copies, waits for them, and re-layouts: 49.9 us -> none  [the longest x32 31.1 us: sub_block(): lax.dynamic_slice_in_dim(bin_codes, 0 + block_index * sub_width, sub_widt...]
    pmax x1 -> x0, blocking collectives: 38.8 us -> none  [local(): best_gain = lax.pmax(best_local, ('rows', 'feat'))]
    ppermute x0 -> x16, starting transfers between devices: none -> 22.2 us  [the longest x12 18.3 us: local(): lax.ppermute(mine[way], 'rows', [(i, i ^ 2 * way) for i in range(owners)])]
    another operation x1 -> x0, loops' own time: 22.1 us -> none  [local(): lax.map(sub_block, jnp.arange(feat_local // sub_width, dtype=jnp.int32))]
    unnamed x3 -> x40, local copies, waits for them, and re-layouts: 9.58 us -> 3.31 us
  transfers between devices with their start and end apart: 0 -> 16, of which waited for: 0 -> 0; matrix products, arithmetic and copies ran while one was open for 0% -> 1% of each run, Pallas kernels for 0% -> 51%
where the time goes in v1:
time: 131 us
  Pallas kernels  89.9 us (69%)
  starting transfers between devices  22.2 us (17%)
  blocking collectives  11.5 us (9%)
  local copies, waits for them, and re-layouts  4.59 us (4%)
  other arithmetic  1.89 us (1%)
    pallas_call x8, Pallas kernels, histogram(): pl.pallas_call(functools.partial(histogram_kernel, add), grid_spec=pltpu....  66.8 us
    ppermute x12, starting transfers between devices, local(): lax.ppermute(mine[way], 'rows', [(i, i ^ 2 * way) for i in range(owners)])  18.3 us
    pallas_call x1, Pallas kernels, pack(): pl.pallas_call(functools.partial(pack_kernel, steps, blocks), grid_spec=p...  12.6 us
    all_to_all x1, blocking collectives, local(): best = lax.all_to_all(best, ('rows', 'feat'), 0, 0, tiled=True)  11.5 us
    pallas_call x4, Pallas kernels, gain(): pl.pallas_call(functools.partial(gain_kernel, count), grid=(1,), in_specs...  10.5 us
    ppermute x4, starting transfers between devices, to_partner(): lax.ppermute(histogram(info, table, weight, owners, chunk, range(base, ba...  3.88 us
    unnamed x40, local copies, waits for them, and re-layouts  3.31 us
  transfers between devices with their start and end apart: 16, of which 0 were waited for; matrix products, arithmetic and copies ran while one was open for 1% of the time, Pallas kernels for 51%

profile of v1, /device:TPU:0, one launch (start us, length us, event | category | flops | bytes accessed | tf_op | source)
XLA Modules:
  0.0 130.9 jit_solution(10838454017171133715)
XLA Ops:
  0.6 1.3 %maximum_convert_fusion.stats_ref = f32[2,32,128]{2,1,0:T(8,128)} fusion(bf16[1,32,128]{2,1,0:T(8,128)(2,1)} %bitcast.8, bf16[1,32,128]{2,1,0:T(8,128)(2,1)} %bitcast.9), kind=kLoop, calls=%fused_computation | loop fusion | flops 16384 | bytes 49152 | tf_op jit(solution)/shard_map/convert_element_type | solution.py:330
  2.0 12.6 %shard_map.68 = (bf16[512,5120]{1,0:T(8,128)(2,1)}, bf16[3,16,5120]{2,1,0:T(8,128)(2,1)}, s32[8]{0:T(128)}) custom-call(s32[1]{0:T(128)} %bitcast.pos_ref, s32[32]{0:T(128)} %leaf_ref.1, s32[32]{0:T(128)} %rows_ref.1, s32[4096,512]{1,0:T(8,128)} %codes_ref.1, f32[2,32,128]{2,1,0:T(8,128)} %maximum_convert_fusion.stats_ref), custom_call_target="tpu_custom_call" | custom-call | flops 4294967296 | bytes 16777216 | tf_op jit(solution)/shard_map/pallas_call | solution.py:119
  14.6 8.3 %shard_map.75 = f32[4,2,2,3,8,256]{5,4,3,2,1,0:T(8,128)} custom-call(s32[8]{0:T(128)} %get-tuple-element.29.refs_0_, bf16[512,5120]{1,0:T(8,128)(2,1)} %get-tuple-element.30.refs_1_.refs_2_.refs_3_.refs_4_, bf16[512,5120]{1,0:T(8,128)(2,1)} %get-tuple-element.30.refs_1_.refs_2_.refs_3_.refs_4_, ...), custom_call_target="tpu_custom_call" | custom-call | flops 6442450944 | bytes 4194304 | tf_op jit(solution)/shard_map/pallas_call | solution.py:226
  22.9 2.4 %collective-permute-start.12 = (f32[4,2,2,3,8,256]{5,4,3,2,1,0:T(8,128)}, f32[4,2,2,3,8,256]{5,4,3,2,1,0:T(8,128)S(1)}, u32[]{:S(2)}, u32[]{:S(2)}) collective-permute-start(f32[4,2,2,3,8,256]{5,4,3,2,1,0:T(8,128)} %shard_map.75), channel_id=1, source_target_pairs={{0,4},{4,0},{8,12},{12,8},{16,20},{20,16},{24,28},{28,24},{1,5},{5... | collective-permute-start | bytes 1179656 | tf_op jit(solution)/shard_map/ppermute | solution.py:341
  25.2 8.3 %shard_map.73 = f32[4,2,2,3,8,256]{5,4,3,2,1,0:T(8,128)} custom-call(s32[8]{0:T(128)} %get-tuple-element.29.refs_0_, bf16[512,5120]{1,0:T(8,128)(2,1)} %get-tuple-element.30.refs_1_.refs_2_.refs_3_.refs_4_, bf16[512,5120]{1,0:T(8,128)(2,1)} %get-tuple-element.30.refs_1_.refs_2_.refs_3_.refs_4_, ...), custom_call_target="tpu_custom_call" | custom-call | flops 6442450944 | bytes 4194304 | tf_op jit(solution)/shard_map/pallas_call | solution.py:226
  33.5 0.0 collective-permute-start.8
  33.5 8.3 %shard_map.71 = f32[4,2,2,3,8,256]{5,4,3,2,1,0:T(8,128)} custom-call(s32[8]{0:T(128)} %get-tuple-element.29.refs_0_, bf16[512,5120]{1,0:T(8,128)(2,1)} %get-tuple-element.30.refs_1_.refs_2_.refs_3_.refs_4_, bf16[512,5120]{1,0:T(8,128)(2,1)} %get-tuple-element.30.refs_1_.refs_2_.refs_3_.refs_4_, ...), custom_call_target="tpu_custom_call" | custom-call | flops 6442450944 | bytes 4194304 | tf_op jit(solution)/shard_map/pallas_call | solution.py:226
  41.8 1.5 %collective-permute-start.4 = (f32[4,2,2,3,8,256]{5,4,3,2,1,0:T(8,128)}, f32[4,2,2,3,8,256]{5,4,3,2,1,0:T(8,128)S(1)}, u32[]{:S(2)}, u32[]{:S(2)}) collective-permute-start(f32[4,2,2,3,8,256]{5,4,3,2,1,0:T(8,128)} %shard_map.71), channel_id=1, source_target_pairs={{0,4},{4,0},{8,12},{12,8},{16,20},{20,16},{24,28},{28,24},{1,5},{5... | collective-permute-start | bytes 1179656 | tf_op jit(solution)/shard_map/ppermute | solution.py:341
  43.3 8.5 %shard_map.69 = f32[4,2,2,3,8,256]{5,4,3,2,1,0:T(8,128)} custom-call(s32[8]{0:T(128)} %get-tuple-element.29.refs_0_, bf16[512,5120]{1,0:T(8,128)(2,1)} %get-tuple-element.30.refs_1_.refs_2_.refs_3_.refs_4_, bf16[512,5120]{1,0:T(8,128)(2,1)} %get-tuple-element.30.refs_1_.refs_2_.refs_3_.refs_4_, ...), custom_call_target="tpu_custom_call" | custom-call | flops 6442450944 | bytes 4194304 | tf_op jit(solution)/shard_map/pallas_call | solution.py:226
  51.8 0.0 collective-permute-start
  51.8 0.0 collective-permute-done.12.refs_6_
  51.8 0.7 copy-done.15
  52.6 8.3 %shard_map.76 = (f32[2,2,3,8,256]{4,3,2,1,0:T(8,128)}, f32[2,2,3,8,256]{4,3,2,1,0:T(8,128)}, f32[2,2,3,8,256]{4,3,2,1,0:T(8,128)}, f32[2,2,3,8,256]{4,3,2,1,0:T(8,128)}) custom-call(s32[8]{0:T(128)} %get-tuple-element.29.refs_0_, bf16[512,5120]{1,0:T(8,128)(2,1)} %get-tuple-element.30.refs_1_.refs_2_.refs_3_.refs_4_, ...), custom_call_target="tpu_custom_call" | custom-call | flops 6442450944 | bytes 4194304 | tf_op jit(solution)/shard_map/pallas_call | solution.py:226
  60.9 2.0 %collective-permute-start.13 = (f32[2,2,3,8,256]{4,3,2,1,0:T(8,128)}, f32[2,2,3,8,256]{4,3,2,1,0:T(8,128)S(1)}, u32[]{:S(2)}, u32[]{:S(2)}) collective-permute-start(f32[2,2,3,8,256]{4,3,2,1,0:T(8,128)} %get-tuple-element.45), channel_id=1, source_target_pairs={{0,8},{4,12},{8,0},{12,4},{16,24},{20,28},{24,16},{28,20},{1,9},{5... | collective-permute-start | bytes 294920 | tf_op jit(solution)/shard_map/ppermute | solution.py:358
  62.9 3.7 %collective-permute-start.14 = (f32[2,2,3,8,256]{4,3,2,1,0:T(8,128)}, f32[2,2,3,8,256]{4,3,2,1,0:T(8,128)S(1)}, u32[]{:S(2)}, u32[]{:S(2)}) collective-permute-start(f32[2,2,3,8,256]{4,3,2,1,0:T(8,128)} %get-tuple-element.46), channel_id=1, source_target_pairs={{0,16},{4,20},{8,24},{12,28},{16,0},{20,4},{24,8},{28,12},{1,17},{... | collective-permute-start | bytes 294920 | tf_op jit(solution)/shard_map/ppermute | solution.py:358
  66.6 0.0 collective-permute-done.8.refs_6_
  66.6 0.0 collective-permute-start.15
  66.6 0.7 copy-done.14
  67.3 8.3 %shard_map.74 = (f32[2,2,3,8,256]{4,3,2,1,0:T(8,128)}, f32[2,2,3,8,256]{4,3,2,1,0:T(8,128)}, f32[2,2,3,8,256]{4,3,2,1,0:T(8,128)}, f32[2,2,3,8,256]{4,3,2,1,0:T(8,128)}) custom-call(s32[8]{0:T(128)} %get-tuple-element.29.refs_0_, bf16[512,5120]{1,0:T(8,128)(2,1)} %get-tuple-element.30.refs_1_.refs_2_.refs_3_.refs_4_, ...), custom_call_target="tpu_custom_call" | custom-call | flops 6442450944 | bytes 4194304 | tf_op jit(solution)/shard_map/pallas_call | solution.py:226
  75.6 0.0 collective-permute-done.4.refs_6_
  75.7 0.3 collective-permute-start.10
  76.0 0.4 copy-done.13
  76.4 8.3 %shard_map.72 = (f32[2,2,3,8,256]{4,3,2,1,0:T(8,128)}, f32[2,2,3,8,256]{4,3,2,1,0:T(8,128)}, f32[2,2,3,8,256]{4,3,2,1,0:T(8,128)}, f32[2,2,3,8,256]{4,3,2,1,0:T(8,128)}) custom-call(s32[8]{0:T(128)} %get-tuple-element.29.refs_0_, bf16[512,5120]{1,0:T(8,128)(2,1)} %get-tuple-element.30.refs_1_.refs_2_.refs_3_.refs_4_, ...), custom_call_target="tpu_custom_call" | custom-call | flops 6442450944 | bytes 4194304 | tf_op jit(solution)/shard_map/pallas_call | solution.py:226
  84.7 0.0 collective-permute-done.refs_6_
  84.7 0.0 copy-done.19
  84.7 3.1 %collective-permute-start.11 = (f32[2,2,3,8,256]{4,3,2,1,0:T(8,128)S(1)}, f32[2,2,3,8,256]{4,3,2,1,0:T(8,128)S(1)}, u32[]{:S(2)}, u32[]{:S(2)}) collective-permute-start(f32[2,2,3,8,256]{4,3,2,1,0:T(8,128)S(1)} %copy-done.19), channel_id=1, source_target_pairs={{0,24},{4,28},{8,16},{12,20},{16,8},{20,12},{24,0},{28,4},{1,25},{... | collective-permute-start | bytes 294920 | tf_op jit(solution)/shard_map/ppermute | solution.py:358
  87.9 0.0 collective-permute-done.13.refs_1_
  87.9 0.1 collective-permute-start.9
  88.0 0.0 collective-permute-done.14.refs_2_
  88.0 2.0 %collective-permute-start.5 = (f32[2,2,3,8,256]{4,3,2,1,0:T(8,128)}, f32[2,2,3,8,256]{4,3,2,1,0:T(8,128)S(1)}, u32[]{:S(2)}, u32[]{:S(2)}) collective-permute-start(f32[2,2,3,8,256]{4,3,2,1,0:T(8,128)} %get-tuple-element.37), channel_id=1, source_target_pairs={{0,8},{4,12},{8,0},{12,4},{16,24},{20,28},{24,16},{28,20},{1,9},{5... | collective-permute-start | bytes 294920 | tf_op jit(solution)/shard_map/ppermute | solution.py:358
  90.0 0.0 copy-done.12
  90.0 8.5 %shard_map.70 = (f32[2,2,3,8,256]{4,3,2,1,0:T(8,128)}, f32[2,2,3,8,256]{4,3,2,1,0:T(8,128)}, f32[2,2,3,8,256]{4,3,2,1,0:T(8,128)}, f32[2,2,3,8,256]{4,3,2,1,0:T(8,128)}) custom-call(s32[8]{0:T(128)} %get-tuple-element.29.refs_0_, bf16[512,5120]{1,0:T(8,128)(2,1)} %get-tuple-element.30.refs_1_.refs_2_.refs_3_.refs_4_, ...), custom_call_target="tpu_custom_call" | custom-call | flops 6442450944 | bytes 4194304 | tf_op jit(solution)/shard_map/pallas_call | solution.py:226
  98.6 0.0 copy-done
  98.6 0.0 collective-permute-done.15.refs_3_
  98.6 0.0 copy-start.2
  98.6 0.0 copy-done.17
  98.6 0.9 collective-permute-start.6
  99.5 0.0 collective-permute-done.10.refs_2_
  99.5 0.0 copy-done.16
  99.5 1.7 %collective-permute-start.7 = (f32[2,2,3,8,256]{4,3,2,1,0:T(8,128)S(1)}, f32[2,2,3,8,256]{4,3,2,1,0:T(8,128)S(1)}, u32[]{:S(2)}, u32[]{:S(2)}) collective-permute-start(f32[2,2,3,8,256]{4,3,2,1,0:T(8,128)S(1)} %copy-done.16), channel_id=1, source_target_pairs={{0,24},{4,28},{8,16},{12,20},{16,8},{20,12},{24,0},{28,4},{1,25},{... | collective-permute-start | bytes 294920 | tf_op jit(solution)/shard_map/ppermute | solution.py:358
  101.2 0.0 collective-permute-done.11.refs_3_
  101.2 1.0 collective-permute-start.1
  102.2 0.0 collective-permute-done.9.refs_1_
  102.2 1.7 %collective-permute-start.2 = (f32[2,2,3,8,256]{4,3,2,1,0:T(8,128)}, f32[2,2,3,8,256]{4,3,2,1,0:T(8,128)S(1)}, u32[]{:S(2)}, u32[]{:S(2)}) collective-permute-start(f32[2,2,3,8,256]{4,3,2,1,0:T(8,128)} %get-tuple-element.34), channel_id=1, source_target_pairs={{0,16},{4,20},{8,24},{12,28},{16,0},{20,4},{24,8},{28,12},{1,17},{... | collective-permute-start | bytes 294920 | tf_op jit(solution)/shard_map/ppermute | solution.py:358
  104.0 0.0 collective-permute-done.5.refs_1_
  104.0 1.7 %collective-permute-start.3 = (f32[2,2,3,8,256]{4,3,2,1,0:T(8,128)}, f32[2,2,3,8,256]{4,3,2,1,0:T(8,128)S(1)}, u32[]{:S(2)}, u32[]{:S(2)}) collective-permute-start(f32[2,2,3,8,256]{4,3,2,1,0:T(8,128)} %get-tuple-element.35), channel_id=1, source_target_pairs={{0,24},{4,28},{8,16},{12,20},{16,8},{20,12},{24,0},{28,4},{1,25},{... | collective-permute-start | bytes 294920 | tf_op jit(solution)/shard_map/ppermute | solution.py:358
  105.6 0.7 broadcast_in_dim.10.refs_4_
  106.3 0.6 broadcast_in_dim.11.refs_5_
  106.9 2.6 %shard_map.77 = (f32[2,64,256]{2,1,0:T(8,128)}, f32[32,128]{1,0:T(8,128)}) custom-call(f32[2,2,3,8,256]{4,3,2,1,0:T(8,128)} %get-tuple-element.44.refs_0_, f32[2,2,3,8,256]{4,3,2,1,0:T(8,128)} %copy-done, f32[2,2,3,8,256]{4,3,2,1,0:T(8,128)} %copy-done.1, f32[2,2,3,8,256]{4,3,2,1,0:T(8,128)} %copy-done.2, ...), custom_call_target="tpu_custom_call", output_to_operand_aliasing={{0}: (4, {}), {1}: (5, {})} | custom-call | tf_op jit(solution)/shard_map/pallas_call | solution.py:308
  109.6 2.6 %shard_map.78 = (f32[2,64,256]{2,1,0:T(8,128)}, f32[32,128]{1,0:T(8,128)}) custom-call(f32[2,2,3,8,256]{4,3,2,1,0:T(8,128)} %get-tuple-element.40.refs_0_, f32[2,2,3,8,256]{4,3,2,1,0:T(8,128)} %copy-done.6, f32[2,2,3,8,256]{4,3,2,1,0:T(8,128)} %copy-done.3, f32[2,2,3,8,256]{4,3,2,1,0:T(8,128)} %copy-done.5, ...), custom_call_target="tpu_custom_call", output_to_operand_aliasing={{0}: (4, {}), {1}: (5, {})} | custom-call | tf_op jit(solution)/shard_map/pallas_call | solution.py:308
  112.2 0.0 collective-permute-done.6.refs_2_
  112.2 0.0 collective-permute-done.7.refs_3_
  112.2 0.6 copy-done.8
  112.8 0.0 copy-done.10
  112.9 2.6 %shard_map.79 = (f32[2,64,256]{2,1,0:T(8,128)}, f32[32,128]{1,0:T(8,128)}) custom-call(f32[2,2,3,8,256]{4,3,2,1,0:T(8,128)} %get-tuple-element.36.refs_0_, f32[2,2,3,8,256]{4,3,2,1,0:T(8,128)} %copy-done.4, f32[2,2,3,8,256]{4,3,2,1,0:T(8,128)} %copy-done.8, f32[2,2,3,8,256]{4,3,2,1,0:T(8,128)} %copy-done.10, ...), custom_call_target="tpu_custom_call", output_to_operand_aliasing={{0}: (4, {}), {1}: (5, {})} | custom-call | tf_op jit(solution)/shard_map/pallas_call | solution.py:308
  115.5 0.0 collective-permute-done.1.refs_1_
  115.5 0.0 collective-permute-done.2.refs_2_
  115.5 0.0 collective-permute-done.3.refs_3_
  115.5 0.6 copy-done.7
  116.1 0.0 copy-done.9
  116.2 0.0 copy-done.11
  116.2 2.6 %shard_map.80 = (f32[2,64,256]{2,1,0:T(8,128)}, f32[32,128]{1,0:T(8,128)}) custom-call(f32[2,2,3,8,256]{4,3,2,1,0:T(8,128)} %get-tuple-element.32.refs_0_, f32[2,2,3,8,256]{4,3,2,1,0:T(8,128)} %copy-done.7, f32[2,2,3,8,256]{4,3,2,1,0:T(8,128)} %copy-done.9, f32[2,2,3,8,256]{4,3,2,1,0:T(8,128)} %copy-done.11, ...), custom_call_target="tpu_custom_call", output_to_operand_aliasing={{0}: (4, {}), {1}: (5, {})} | custom-call | tf_op jit(solution)/shard_map/pallas_call | solution.py:308
  118.8 11.5 %all_to_all.9 = f32[32,1,128]{2,1,0:T(1,128)S(1)} all-to-all(f32[32,1,128]{2,1,0:T(1,128)} %bitcast.7), channel_id=1, replica_groups=mesh['rows'=8,'feat'=4] {'rows','feat'}, dimensions={0} | all-to-all | bytes 32768 | tf_op jit(solution)/shard_map/all_to_all | solution.py:360
  130.3 0.6 reduce_max.9
  (26 shorter events, 0.0 us)
Async XLA Ops:
  22.9 28.9 %collective-permute-start.12 = (f32[4,2,2,3,8,256]{5,4,3,2,1,0:T(8,128)}, f32[4,2,2,3,8,256]{5,4,3,2,1,0:T(8,128)S(1)}, u32[]{:S(2)}, u32[]{:S(2)}) collective-permute-start(f32[4,2,2,3,8,256]{5,4,3,2,1,0:T(8,128)} %shard_map.75), channel_id=1, source_target_pairs={{0,4},{4,0},{8,12},{12,8},{16,20},{20,16},{24,28},{28,24},{1,5},{5... | collective-permute-start | bytes 1179656 | tf_op jit(solution)/shard_map/ppermute | solution.py:341
  33.5 33.0 %collective-permute-start.8 = (f32[4,2,2,3,8,256]{5,4,3,2,1,0:T(8,128)}, f32[4,2,2,3,8,256]{5,4,3,2,1,0:T(8,128)S(1)}, u32[]{:S(2)}, u32[]{:S(2)}) collective-permute-start(f32[4,2,2,3,8,256]{5,4,3,2,1,0:T(8,128)} %shard_map.73), channel_id=1, source_target_pairs={{0,4},{4,0},{8,12},{12,8},{16,20},{20,16},{24,28},{28,24},{1,5},{5... | collective-permute-start | bytes 1179656 | tf_op jit(solution)/shard_map/ppermute | solution.py:341
  41.8 33.8 %collective-permute-start.4 = (f32[4,2,2,3,8,256]{5,4,3,2,1,0:T(8,128)}, f32[4,2,2,3,8,256]{5,4,3,2,1,0:T(8,128)S(1)}, u32[]{:S(2)}, u32[]{:S(2)}) collective-permute-start(f32[4,2,2,3,8,256]{5,4,3,2,1,0:T(8,128)} %shard_map.71), channel_id=1, source_target_pairs={{0,4},{4,0},{8,12},{12,8},{16,20},{20,16},{24,28},{28,24},{1,5},{5... | collective-permute-start | bytes 1179656 | tf_op jit(solution)/shard_map/ppermute | solution.py:341
  51.8 32.9 %collective-permute-start = (f32[4,2,2,3,8,256]{5,4,3,2,1,0:T(8,128)}, f32[4,2,2,3,8,256]{5,4,3,2,1,0:T(8,128)S(1)}, u32[]{:S(2)}, u32[]{:S(2)}) collective-permute-start(f32[4,2,2,3,8,256]{5,4,3,2,1,0:T(8,128)} %shard_map.69), channel_id=1, source_target_pairs={{0,4},{4,0},{8,12},{12,8},{16,20},{20,16},{24,28},{28,24},{1,5},{5... | collective-permute-start | bytes 1179656 | tf_op jit(solution)/shard_map/ppermute | solution.py:341
  51.8 0.8 copy-start.15
  60.9 27.0 %collective-permute-start.13 = (f32[2,2,3,8,256]{4,3,2,1,0:T(8,128)}, f32[2,2,3,8,256]{4,3,2,1,0:T(8,128)S(1)}, u32[]{:S(2)}, u32[]{:S(2)}) collective-permute-start(f32[2,2,3,8,256]{4,3,2,1,0:T(8,128)} %get-tuple-element.45), channel_id=1, source_target_pairs={{0,8},{4,12},{8,0},{12,4},{16,24},{20,28},{24,16},{28,20},{1,9},{5... | collective-permute-start | bytes 294920 | tf_op jit(solution)/shard_map/ppermute | solution.py:358
  62.9 25.1 %collective-permute-start.14 = (f32[2,2,3,8,256]{4,3,2,1,0:T(8,128)}, f32[2,2,3,8,256]{4,3,2,1,0:T(8,128)S(1)}, u32[]{:S(2)}, u32[]{:S(2)}) collective-permute-start(f32[2,2,3,8,256]{4,3,2,1,0:T(8,128)} %get-tuple-element.46), channel_id=1, source_target_pairs={{0,16},{4,20},{8,24},{12,28},{16,0},{20,4},{24,8},{28,12},{1,17},{... | collective-permute-start | bytes 294920 | tf_op jit(solution)/shard_map/ppermute | solution.py:358
  66.6 0.7 copy-start.14
  66.6 32.0 %collective-permute-start.15 = (f32[2,2,3,8,256]{4,3,2,1,0:T(8,128)}, f32[2,2,3,8,256]{4,3,2,1,0:T(8,128)S(1)}, u32[]{:S(2)}, u32[]{:S(2)}) collective-permute-start(f32[2,2,3,8,256]{4,3,2,1,0:T(8,128)} %get-tuple-element.47), channel_id=1, source_target_pairs={{0,24},{4,28},{8,16},{12,20},{16,8},{20,12},{24,0},{28,4},{1,25},{... | collective-permute-start | bytes 294920 | tf_op jit(solution)/shard_map/ppermute | solution.py:358
  75.6 0.8 copy-start.13
  75.6 9.1 %copy-start.19 = (f32[2,2,3,8,256]{4,3,2,1,0:T(8,128)S(1)}, f32[2,2,3,8,256]{4,3,2,1,0:T(8,128)}, u32[]{:S(2)}) copy-start(f32[2,2,3,8,256]{4,3,2,1,0:T(8,128)} %get-tuple-element.43) | copy-start | bytes 294916
  75.6 12.2 %copy-start.18 = (f32[2,2,3,8,256]{4,3,2,1,0:T(8,128)S(1)}, f32[2,2,3,8,256]{4,3,2,1,0:T(8,128)}, u32[]{:S(2)}) copy-start(f32[2,2,3,8,256]{4,3,2,1,0:T(8,128)} %get-tuple-element.41) | copy-start | bytes 294916
  75.7 23.8 %collective-permute-start.10 = (f32[2,2,3,8,256]{4,3,2,1,0:T(8,128)}, f32[2,2,3,8,256]{4,3,2,1,0:T(8,128)S(1)}, u32[]{:S(2)}, u32[]{:S(2)}) collective-permute-start(f32[2,2,3,8,256]{4,3,2,1,0:T(8,128)} %get-tuple-element.42), channel_id=1, source_target_pairs={{0,16},{4,20},{8,24},{12,28},{16,0},{20,4},{24,8},{28,12},{1,17},{... | collective-permute-start | bytes 294920 | tf_op jit(solution)/shard_map/ppermute | solution.py:358
  84.7 5.3 %copy-start.12 = (f32[4,2,2,3,8,256]{5,4,3,2,1,0:T(8,128)}, f32[4,2,2,3,8,256]{5,4,3,2,1,0:T(8,128)S(1)}, u32[]{:S(2)}) copy-start(f32[4,2,2,3,8,256]{5,4,3,2,1,0:T(8,128)S(1)} %collective-permute-done.refs_6_) | copy-start | bytes 1179652
  84.7 16.5 %collective-permute-start.11 = (f32[2,2,3,8,256]{4,3,2,1,0:T(8,128)S(1)}, f32[2,2,3,8,256]{4,3,2,1,0:T(8,128)S(1)}, u32[]{:S(2)}, u32[]{:S(2)}) collective-permute-start(f32[2,2,3,8,256]{4,3,2,1,0:T(8,128)S(1)} %copy-done.19), channel_id=1, source_target_pairs={{0,24},{4,28},{8,16},{12,20},{16,8},{20,12},{24,0},{28,4},{1,25},{... | collective-permute-start | bytes 294920 | tf_op jit(solution)/shard_map/ppermute | solution.py:358
  87.9 10.7 %copy-start = (f32[2,2,3,8,256]{4,3,2,1,0:T(8,128)}, f32[2,2,3,8,256]{4,3,2,1,0:T(8,128)S(1)}, u32[]{:S(2)}) copy-start(f32[2,2,3,8,256]{4,3,2,1,0:T(8,128)S(1)} %collective-permute-done.13.refs_1_) | copy-start | bytes 294916
  87.9 14.4 %collective-permute-start.9 = (f32[2,2,3,8,256]{4,3,2,1,0:T(8,128)S(1)}, f32[2,2,3,8,256]{4,3,2,1,0:T(8,128)S(1)}, u32[]{:S(2)}, u32[]{:S(2)}) collective-permute-start(f32[2,2,3,8,256]{4,3,2,1,0:T(8,128)S(1)} %copy-done.18), channel_id=1, source_target_pairs={{0,8},{4,12},{8,0},{12,4},{16,24},{20,28},{24,16},{28,20},{1,9},{5... | collective-permute-start | bytes 294920 | tf_op jit(solution)/shard_map/ppermute | solution.py:358
  88.0 10.6 %copy-start.1 = (f32[2,2,3,8,256]{4,3,2,1,0:T(8,128)}, f32[2,2,3,8,256]{4,3,2,1,0:T(8,128)S(1)}, u32[]{:S(2)}) copy-start(f32[2,2,3,8,256]{4,3,2,1,0:T(8,128)S(1)} %collective-permute-done.14.refs_2_) | copy-start | bytes 294916
  88.0 10.6 %copy-start.17 = (f32[2,2,3,8,256]{4,3,2,1,0:T(8,128)S(1)}, f32[2,2,3,8,256]{4,3,2,1,0:T(8,128)}, u32[]{:S(2)}) copy-start(f32[2,2,3,8,256]{4,3,2,1,0:T(8,128)} %get-tuple-element.38) | copy-start | bytes 294916
  88.0 11.5 %copy-start.16 = (f32[2,2,3,8,256]{4,3,2,1,0:T(8,128)S(1)}, f32[2,2,3,8,256]{4,3,2,1,0:T(8,128)}, u32[]{:S(2)}) copy-start(f32[2,2,3,8,256]{4,3,2,1,0:T(8,128)} %get-tuple-element.39) | copy-start | bytes 294916
  88.0 16.0 %collective-permute-start.5 = (f32[2,2,3,8,256]{4,3,2,1,0:T(8,128)}, f32[2,2,3,8,256]{4,3,2,1,0:T(8,128)S(1)}, u32[]{:S(2)}, u32[]{:S(2)}) collective-permute-start(f32[2,2,3,8,256]{4,3,2,1,0:T(8,128)} %get-tuple-element.37), channel_id=1, source_target_pairs={{0,8},{4,12},{8,0},{12,4},{16,24},{20,28},{24,16},{28,20},{1,9},{5... | collective-permute-start | bytes 294920 | tf_op jit(solution)/shard_map/ppermute | solution.py:358
  98.6 8.3 %copy-start.2 = (f32[2,2,3,8,256]{4,3,2,1,0:T(8,128)}, f32[2,2,3,8,256]{4,3,2,1,0:T(8,128)S(1)}, u32[]{:S(2)}) copy-start(f32[2,2,3,8,256]{4,3,2,1,0:T(8,128)S(1)} %collective-permute-done.15.refs_3_) | copy-start | bytes 294916
  98.6 13.6 %collective-permute-start.6 = (f32[2,2,3,8,256]{4,3,2,1,0:T(8,128)S(1)}, f32[2,2,3,8,256]{4,3,2,1,0:T(8,128)S(1)}, u32[]{:S(2)}, u32[]{:S(2)}) collective-permute-start(f32[2,2,3,8,256]{4,3,2,1,0:T(8,128)S(1)} %copy-done.17), channel_id=1, source_target_pairs={{0,16},{4,20},{8,24},{12,28},{16,0},{20,4},{24,8},{28,12},{1,17},{... | collective-permute-start | bytes 294920 | tf_op jit(solution)/shard_map/ppermute | solution.py:358
  99.5 10.1 %copy-start.3 = (f32[2,2,3,8,256]{4,3,2,1,0:T(8,128)}, f32[2,2,3,8,256]{4,3,2,1,0:T(8,128)S(1)}, u32[]{:S(2)}) copy-start(f32[2,2,3,8,256]{4,3,2,1,0:T(8,128)S(1)} %collective-permute-done.10.refs_2_) | copy-start | bytes 294916
  99.5 12.7 %collective-permute-start.7 = (f32[2,2,3,8,256]{4,3,2,1,0:T(8,128)S(1)}, f32[2,2,3,8,256]{4,3,2,1,0:T(8,128)S(1)}, u32[]{:S(2)}, u32[]{:S(2)}) collective-permute-start(f32[2,2,3,8,256]{4,3,2,1,0:T(8,128)S(1)} %copy-done.16), channel_id=1, source_target_pairs={{0,24},{4,28},{8,16},{12,20},{16,8},{20,12},{24,0},{28,4},{1,25},{... | collective-permute-start | bytes 294920 | tf_op jit(solution)/shard_map/ppermute | solution.py:358
  101.2 8.3 %copy-start.5 = (f32[2,2,3,8,256]{4,3,2,1,0:T(8,128)}, f32[2,2,3,8,256]{4,3,2,1,0:T(8,128)S(1)}, u32[]{:S(2)}) copy-start(f32[2,2,3,8,256]{4,3,2,1,0:T(8,128)S(1)} %collective-permute-done.11.refs_3_) | copy-start | bytes 294916
  101.2 14.2 %collective-permute-start.1 = (f32[2,2,3,8,256]{4,3,2,1,0:T(8,128)}, f32[2,2,3,8,256]{4,3,2,1,0:T(8,128)S(1)}, u32[]{:S(2)}, u32[]{:S(2)}) collective-permute-start(f32[2,2,3,8,256]{4,3,2,1,0:T(8,128)} %get-tuple-element.33), channel_id=1, source_target_pairs={{0,8},{4,12},{8,0},{12,4},{16,24},{20,28},{24,16},{28,20},{1,9},{5... | collective-permute-start | bytes 294920 | tf_op jit(solution)/shard_map/ppermute | solution.py:358
  102.2 7.3 %copy-start.6 = (f32[2,2,3,8,256]{4,3,2,1,0:T(8,128)}, f32[2,2,3,8,256]{4,3,2,1,0:T(8,128)S(1)}, u32[]{:S(2)}) copy-start(f32[2,2,3,8,256]{4,3,2,1,0:T(8,128)S(1)} %collective-permute-done.9.refs_1_) | copy-start | bytes 294916
  102.2 13.2 %collective-permute-start.2 = (f32[2,2,3,8,256]{4,3,2,1,0:T(8,128)}, f32[2,2,3,8,256]{4,3,2,1,0:T(8,128)S(1)}, u32[]{:S(2)}, u32[]{:S(2)}) collective-permute-start(f32[2,2,3,8,256]{4,3,2,1,0:T(8,128)} %get-tuple-element.34), channel_id=1, source_target_pairs={{0,16},{4,20},{8,24},{12,28},{16,0},{20,4},{24,8},{28,12},{1,17},{... | collective-permute-start | bytes 294920 | tf_op jit(solution)/shard_map/ppermute | solution.py:358
  104.0 8.2 %copy-start.4 = (f32[2,2,3,8,256]{4,3,2,1,0:T(8,128)}, f32[2,2,3,8,256]{4,3,2,1,0:T(8,128)S(1)}, u32[]{:S(2)}) copy-start(f32[2,2,3,8,256]{4,3,2,1,0:T(8,128)S(1)} %collective-permute-done.5.refs_1_) | copy-start | bytes 294916
  104.0 11.5 %collective-permute-start.3 = (f32[2,2,3,8,256]{4,3,2,1,0:T(8,128)}, f32[2,2,3,8,256]{4,3,2,1,0:T(8,128)S(1)}, u32[]{:S(2)}, u32[]{:S(2)}) collective-permute-start(f32[2,2,3,8,256]{4,3,2,1,0:T(8,128)} %get-tuple-element.35), channel_id=1, source_target_pairs={{0,24},{4,28},{8,16},{12,20},{16,8},{20,12},{24,0},{28,4},{1,25},{... | collective-permute-start | bytes 294920 | tf_op jit(solution)/shard_map/ppermute | solution.py:358
  112.2 0.6 copy-start.8
  112.2 0.7 copy-start.10
  115.5 0.6 copy-start.7
  115.5 0.7 copy-start.9
  115.5 0.7 copy-start.11
